TPU v7x, 32 devices: a whole 2x2x4 slice. The times are simulated.
32 devices in a mesh: dp: 16 (over z, y, x), factor: 2 (over core).
Axes of the slice: x: 2, y: 2, z: 4, core: 2. Of those that a mesh axis runs over, the one named last changes fastest.
Arguments:
- layer_inputs: bfloat16 [16384, 5120], P('dp', 'factor'), may hold values from -64 to 64
- out_grads: bfloat16 [16384, 5120], P('dp', 'factor'), may hold values from -64 to 64
- weight_grad: bfloat16 [5120, 5120], P('dp', 'factor'), may hold values from -32 to 32
- left_inv: float32 [5120, 5120], P('dp', 'factor'), may hold values from -4 to 10, as said below
- right_inv: float32 [5120, 5120], P('factor', 'dp'), may hold values from -4 to 10, as said below
Outputs:
- precond_grad: bfloat16 [5120, 5120], P('dp', 'factor')
- new_left: float32 [5120, 5120], P('dp', 'factor')
- new_right: float32 [5120, 5120], P('factor', 'dp')
Inputs may be any that keep to these rules, and one draw needn't show every extreme that they name: `left_inv`: symmetric and positive definite, every eigenvalue 0.1 or more. `right_inv`: symmetric and positive definite, every eigenvalue 0.1 or more.
All inputs are finite; a program needn't handle non-finite values.
Results may differ from a plain program's by a relative error of at most 0.00275.
The roundings to bfloat16 on the way count: a program that leaves them out, or rounds other values in their place, can miss the bound.
Values may be sent and summed in bfloat16 or wider, within the bound.
A program may use at most 128 MiB of HBM per device.

v0:
```python
import jax
import jax.numpy as jnp
from jax import lax
from jax.sharding import PartitionSpec as P

decay = 0.9


def coefficient(quadratic):
    return (1.0 - decay) / (decay * decay * (1.0 + (1.0 - decay) / decay * quadratic))


def per_device(layer_inputs, out_grads, weight_grad, left_inv, right_inv):
    highest = lax.Precision.HIGHEST
    token_count = layer_inputs.shape[0] * lax.axis_size("dp")
    act_local = jnp.sum(layer_inputs, axis=0, dtype=jnp.float32)
    grad_local = jnp.sum(out_grads, axis=0, dtype=jnp.float32)
    act_sums, grad_sums = lax.psum((act_local, grad_local), "dp")
    mean_act = act_sums / token_count
    mean_grad = grad_sums / token_count
    whole_act, whole_grad = (
        lax.all_gather(mean_act, "factor", axis=0, tiled=True),
        lax.all_gather(mean_grad, "factor", axis=0, tiled=True),
    )
    left_rows, left_cols = left_inv.shape
    right_rows, right_cols = right_inv.shape
    data_index = lax.axis_index("dp")
    act_rows = lax.dynamic_slice_in_dim(whole_act, data_index * left_rows, left_rows)
    grad_cols = lax.dynamic_slice_in_dim(whole_grad, data_index * right_cols, right_cols)
    row_terms = jnp.dot(left_inv, mean_act, precision=highest)
    col_terms = jnp.dot(mean_grad, right_inv, precision=highest)
    left_image_rows, right_image_cols = lax.psum((row_terms, col_terms), "factor")
    left_partial = jnp.dot(act_rows, left_inv, precision=highest)
    right_partial = jnp.dot(right_inv, grad_cols, precision=highest)
    left_image_cols, right_image_rows = lax.psum((left_partial, right_partial), "dp")
    left_quad, right_quad = lax.psum(
        (jnp.sum(mean_act * left_image_cols), jnp.sum(mean_grad * right_image_rows)), "factor"
    )
    left_coef = coefficient(left_quad)
    right_coef = coefficient(right_quad)
    new_left = left_inv / decay - left_coef * left_image_rows[:, None] * left_image_cols[None, :]
    new_right = (
        right_inv / decay - right_coef * right_image_rows[:, None] * right_image_cols[None, :]
    )
    left_half = new_left.astype(jnp.bfloat16)
    right_half = new_right.astype(jnp.bfloat16)
    left_wide = lax.all_gather(left_half, "factor", axis=1, tiled=True)
    matched = left_wide
    hidden_sum = jnp.dot(
        matched,
        lax.all_gather(weight_grad, "dp", axis=0, tiled=True),
        preferred_element_type=jnp.float32,
    )
    hidden = hidden_sum.astype(jnp.bfloat16)
    hidden_wide = lax.all_gather(hidden, "factor", axis=1, tiled=True)
    matched = hidden_wide
    precond = lax.dot_general(
        matched,
        lax.all_gather(right_half, "dp", axis=1, tiled=True),
        (((1,), (1,)), ((), ())),
        preferred_element_type=jnp.float32,
    )
    return (precond.astype(jnp.bfloat16), new_left, new_right)


def solution(mesh):
    in_specs = (
        P("dp", "factor"),
        P("dp", "factor"),
        P("dp", "factor"),
        P("dp", "factor"),
        P("factor", "dp"),
    )
    out_specs = (P("dp", "factor"), P("dp", "factor"), P("factor", "dp"))
    return jax.shard_map(
        per_device, mesh=mesh, in_specs=in_specs, out_specs=out_specs, check_vma=False
    )
```

profile of v0, /device:TPU:3, one launch (start us, length us, event | category | flops | bytes accessed | tf_op | source)
XLA Modules:
  0.0 792.2 jit_solution(4838888443683797496)
XLA Ops:
  7.2 0.0 all-gather.7.cloned.1.call-start
  7.2 3.4 convert_reduce_fusion.1
  10.6 0.6 copy-done.3
  11.3 0.8 convert_reduce_fusion
  12.0 58.1 %all-reduce.1 = (f32[2560]{0:T(1024)S(1)}, f32[2560]{0:T(1024)S(1)}) all-reduce(f32[2560]{0:T(1024)S(1)} %convert_reduce_fusion.1, f32[2560]{0:T(1024)S(1)} %convert_reduce_fusion), channel_id=1, replica_groups=mesh['dp'=16,'factor'=2] {'dp'}, use_global_device_ids=true, to_apply=%region_1.0 | all-reduce | flops 5120 | bytes 40960 | tf_op jit(solution)/shard_map/psum | solution.py:18
  70.2 16.0 %all-gather = f32[2,1,2560]{2,1,0:T(1,128)S(1)} all-gather(f32[1,1,2560]{2,1,0:T(1,128)S(1)} %reshape.12), channel_id=1, replica_groups=mesh['dp'=16,'factor'=2] {'factor'}, dimensions={0}, use_global_device_ids=true | all-gather | bytes 30720 | tf_op jit(solution)/shard_map/all_gather | solution.py:22
  86.2 0.1 dynamic_slice.6
  86.3 2.7 convolution_reduce_fusion.3
  89.0 1.7 convolution_reduce_fusion.1
  90.6 1.8 all-gather.1
  92.5 0.1 dynamic_slice.7
  92.5 2.7 convolution_reduce_fusion.2
  95.3 1.7 convolution_reduce_fusion
  97.0 60.0 %all-reduce = (f32[2560]{0:T(1024)S(1)}, f32[2560]{0:T(1024)S(1)}) all-reduce(f32[2560]{0:T(1024)S(1)} %convolution_reduce_fusion.1, f32[2560]{0:T(1024)S(1)} %convolution_reduce_fusion), channel_id=1, replica_groups=mesh['dp'=16,'factor'=2] {'dp'}, use_global_device_ids=true, to_apply=%region_2.0 | all-reduce | flops 5120 | bytes 40960 | tf_op jit(solution)/shard_map/psum | solution.py:35
  157.0 0.6 multiply_reduce_fusion
  157.6 17.1 %all-reduce.2 = (f32[320]{0:T(512)S(1)}, f32[]{:T(128)}, f32[320]{0:T(512)S(1)}, f32[]{:T(128)}) all-reduce(f32[320]{0:T(512)S(1)} %convolution_reduce_fusion.3, f32[]{:T(128)} %get-tuple-element.16, f32[320]{0:T(512)S(1)} %convolution_reduce_fusion.2, f32[]{:T(128)} %get-tuple-element.15), channel_id=1, replica_groups=mesh['dp'=16,'factor'=2] {'factor'}, use_global_device_ids=true, to_apply=%region_5.0 | all-reduce | flops 642 | bytes 5136 | tf_op jit(solution)/shard_map/psum | solution.py:32
  175.4 2.7 fusion.1
  178.1 0.0 all-gather.7.cloned.1.call-update
  178.1 0.0 all-gather.9.cloned.1.call-start
  178.2 0.7 all-gather.9.cloned.1.call-update
  178.9 0.2 all-gather.13.cloned.1.call-start
  179.8 0.2 copy-done.2
  180.0 2.7 fusion
  182.7 0.0 all-gather.13.cloned.1.call-update
  182.8 0.0 all-gather.11.cloned.1.call-start
  182.8 7.3 all-gather.7.cloned.1.call-done
  190.1 284.2 %all-gather.9.cloned.1.call-done = bf16[5120,2560]{1,0:T(8,128)(2,1)} async-done(((bf16[320,2560]{1,0:T(8,128)(2,1)}), bf16[5120,2560]{1,0:T(8,128)(2,1)}) %all-gather.9.cloned.1.call-update) | async-done | bytes 26214416 | tf_op jit(solution)/shard_map/all_gather | solution.py:51
  474.3 15.5 %convolution_convert_fusion.1 = bf16[320,2560]{1,0:T(8,128)(2,1)} fusion(bf16[320,5120]{1,0:T(8,128)(2,1)} %all-gather.7.cloned.1.call-done, bf16[5120,2560]{1,0:T(8,128)(2,1)} %all-gather.9.cloned.1.call-done), kind=kOutput, calls=%fused_computation.3 | convolution fusion | flops 8389427200 | bytes 31129600 | tf_op jit(solution)/shard_map/dot_general | solution.py:49
  489.8 0.0 all-gather.11.cloned.1.call-update
  489.9 266.8 %all-gather.13.cloned.1.call-done = bf16[2560,5120]{0,1:T(8,128)(2,1)} async-done(((bf16[2560,320]{0,1:T(8,128)(2,1)}), bf16[2560,5120]{0,1:T(8,128)(2,1)}) %all-gather.13.cloned.1.call-update) | async-done | bytes 26214416 | tf_op jit(solution)/shard_map/all_gather | solution.py:59
  756.7 13.7 %all-gather.11.cloned.1.call-done = bf16[320,5120]{1,0:T(8,128)(2,1)} async-done(((bf16[320,2560]{1,0:T(8,128)(2,1)}), bf16[320,5120]{1,0:T(8,128)(2,1)}) %all-gather.11.cloned.1.call-update) | async-done | bytes 3276816 | tf_op jit(solution)/shard_map/all_gather | solution.py:55
  770.4 15.3 %convolution_convert_fusion = bf16[320,2560]{1,0:T(8,128)(2,1)} fusion(bf16[320,5120]{1,0:T(8,128)(2,1)} %all-gather.11.cloned.1.call-done, bf16[2560,5120]{0,1:T(8,128)(2,1)} %all-gather.13.cloned.1.call-done), kind=kOutput, calls=%fused_computation.2 | convolution fusion | flops 8389427200 | bytes 31129600 | tf_op jit(solution)/shard_map/dot_general | solution.py:57
  (16 shorter events, 0.1 us)
Async XLA Ops:
  7.2 182.9 %all-gather.7.cloned.1.call-start = ((), (), s32[]{:S(2)}) async-start(), calls=%async_computation | async-start | bytes 4915200 | tf_op jit(solution)/shard_map/all_gather | solution.py:47
  7.2 4.0 copy-start.3
  11.3 75.0 %copy-start = (f32[320,2560]{1,0:T(8,128)S(1)}, f32[320,2560]{1,0:T(8,128)}, u32[]{:S(2)}) copy-start(f32[320,2560]{1,0:T(8,128)} %param.8) | copy-start | bytes 9830404
  86.3 6.3 copy-start.1
  178.1 1.9 copy-start.2
  178.1 296.2 %all-gather.9.cloned.1.call-start = ((), (), s32[]{:S(2)}) async-start(), calls=%async_computation.1 | async-start | bytes 27852800 | tf_op jit(solution)/shard_map/all_gather | solution.py:51
  178.9 577.8 %all-gather.13.cloned.1.call-start = ((), (), s32[]{:S(2)}) async-start(), calls=%async_computation.3 | async-start | bytes 27852800 | tf_op jit(solution)/shard_map/all_gather | solution.py:59
  182.8 587.6 %all-gather.11.cloned.1.call-start = ((), (), s32[]{:S(2)}) async-start(), calls=%async_computation.2 | async-start | bytes 4915200 | tf_op jit(solution)/shard_map/all_gather | solution.py:55
Sparse Core Ops, SparseCore 0:
  178.2 11.7 all-gather.6
  192.8 281.4 all-gather.8
  477.0 279.6 all-gather.12
  758.7 11.6 all-gather.10
where the time goes:
time: 793 us; the launch traced here: 792 us
  waiting for transfers between devices  573 us (72%)
  blocking collectives  153 us (19%)
  matrix products  39.6 us (5%)
  between operations  15.3 us (2%)
  other arithmetic  10.2 us (1%)
    all_gather x1, waiting for transfers between devices, per_device(): lax.all_gather(weight_grad, 'dp', axis=0, tiled=True)  284 us
    all_gather x1, waiting for transfers between devices, per_device(): lax.all_gather(right_half, 'dp', axis=1, tiled=True)  267 us
    psum x1, blocking collectives, per_device(): lax.psum((left_partial, right_partial), 'dp')  60 us
    psum x1, blocking collectives, per_device(): act_sums, grad_sums = lax.psum((act_local, grad_local), 'dp')  58.1 us
    psum x1, blocking collectives, per_device(): lax.psum((row_terms, col_terms), 'factor')  17.1 us
    all_gather x1, blocking collectives, per_device(): lax.all_gather(mean_act, 'factor', axis=0, tiled=True)  16 us
  transfers between devices with their start and end apart: 4, of which 4 were waited for; matrix products, arithmetic and copies ran while one was open for 2% of the time, Pallas kernels for 0%

commit v1 on v0

--- a/solution.py
+++ b/solution.py
@@ -1,6 +1,9 @@
+import functools
 import jax
 import jax.numpy as jnp
 from jax import lax
+from jax.experimental import pallas as pl
+from jax.experimental.pallas import tpu as pltpu
 from jax.sharding import PartitionSpec as P
 
 decay = 0.9
@@ -10,7 +13,7 @@
     return (1.0 - decay) / (decay * decay * (1.0 + (1.0 - decay) / decay * quadratic))
 
 
-def per_device(layer_inputs, out_grads, weight_grad, left_inv, right_inv):
+def gathered(layer_inputs, out_grads, weight_grad, left_inv, right_inv):
     highest = lax.Precision.HIGHEST
     token_count = layer_inputs.shape[0] * lax.axis_size("dp")
     act_local = jnp.sum(layer_inputs, axis=0, dtype=jnp.float32)
@@ -63,6 +66,374 @@
     return (precond.astype(jnp.bfloat16), new_left, new_right)
 
 
+MESH = pl.DeviceIdType.MESH
+
+
+def split(count):
+    inner = 1
+    for size in range(1, count + 1):
+        if count % size == 0 and size * size <= count:
+            inner = size
+    return count // inner, inner
+
+
+def kernel(
+    outer, inner, cores, tokens,
+    sums_ref, w_ref, l_ref, r_ref,
+    out_ref, new_l_ref, new_r_ref,
+    sums_all, mean_all, part_all, image, image_half, columns,
+    l_buf, r_buf, r_half, w_panel, l_panel, r_panel, h_panel, result,
+    load_sem, store_sem,
+    sums_send, mean_send, part_send, w_send, l_send, r_send, h_send, out_send,
+    sums_recv, mean_recv, part_recv, w_recv, l_recv, r_recv, h_recv, out_recv,
+):
+    data = outer * inner
+    count = data * cores
+    plane = inner * cores
+    rows, cols = l_buf.shape
+    width = w_panel.shape[1]
+    me_data = lax.axis_index("dp")
+    me_core = lax.axis_index("factor")
+    me = me_data * cores + me_core
+    me_outer = me_data // inner
+    me_inner = me_data % inner
+
+    def remote(src, dst, send, recv, target_data, target_core):
+        return pltpu.make_async_remote_copy(
+            src_ref=src, dst_ref=dst, send_sem=send, recv_sem=recv,
+            device_id=(target_data, target_core), device_id_type=MESH,
+        )
+
+    def each(total, body):
+        def step(index, carry):
+            body(index)
+            return carry
+
+        lax.fori_loop(0, total, step, 0)
+
+    load_l = pltpu.make_async_copy(l_ref, l_buf, load_sem.at[0])
+    load_r = pltpu.make_async_copy(r_ref, r_buf, load_sem.at[1])
+    load_l.start()
+    load_r.start()
+    sums_all[me_data] = sums_ref[...]
+
+    barrier = pltpu.get_barrier_semaphore()
+
+    def greet(index):
+        target = (me + 1 + index) % count
+        pl.semaphore_signal(
+            barrier, inc=1, device_id=(target // cores, target % cores), device_id_type=MESH
+        )
+
+    each(count - 1, greet)
+    pl.semaphore_wait(barrier, count - 1)
+
+    def sums_copy(index):
+        target = (me_data + 1 + index) % data
+        return remote(
+            sums_all.at[me_data], sums_all.at[me_data],
+            sums_send.at[index], sums_recv, target, me_core,
+        )
+
+    each(data - 1, lambda index: sums_copy(index).start())
+
+    def w_copy(index):
+        target = (me_data + 1 + index) % data
+        return remote(
+            w_ref.at[:, pl.ds(pl.multiple_of((target % inner) * width, width), width)],
+            w_panel.at[pl.ds(pl.multiple_of(me_data * rows, rows), rows), :],
+            w_send.at[index], w_recv, target, me_core,
+        )
+
+    w_own = pltpu.make_async_copy(
+        w_ref.at[:, pl.ds(pl.multiple_of(me_inner * width, width), width)],
+        w_panel.at[pl.ds(pl.multiple_of(me_data * rows, rows), rows), :],
+        w_recv,
+    )
+
+    def start_w():
+        each(data - 1, lambda index: w_copy(index).start())
+        w_own.start()
+
+    start_w()
+
+    some = sums_all.at[pl.ds(0, data - 1)]
+    pltpu.make_async_copy(some, some, sums_recv).wait()
+    mean = jnp.sum(sums_all[...], axis=0) / tokens
+    mean_all[me_core] = mean
+
+    def mean_copy(index):
+        target = (me_core + 1 + index) % cores
+        return remote(
+            mean_all.at[me_core], mean_all.at[me_core],
+            mean_send.at[index], mean_recv, me_data, target,
+        )
+
+    each(cores - 1, lambda index: mean_copy(index).start())
+    load_l.wait()
+    load_r.wait()
+    step = 32
+    for side, buf in enumerate((l_buf, r_buf)):
+
+        def partial(index, side=side, buf=buf):
+            piece = pl.ds(pl.multiple_of(index * step, step), step)
+            total = jnp.sum(
+                buf[piece, :] * mean_all[me_core][side : side + 1, :], axis=1, keepdims=True
+            )
+            columns[side, piece, :] = jnp.broadcast_to(total, (step, 128))
+
+        each(rows // step, partial)
+    part_all[me] = jnp.concatenate(
+        [jnp.transpose(columns[side])[0:1, :] for side in range(2)], axis=0
+    )
+
+    def part_copy(index):
+        target = (me + 1 + index) % count
+        return remote(
+            part_all.at[me], part_all.at[me],
+            part_send.at[index], part_recv, target // cores, target % cores,
+        )
+
+    each(count - 1, lambda index: part_copy(index).start())
+
+    other_means = mean_all.at[pl.ds(0, cores - 1)]
+    pltpu.make_async_copy(other_means, other_means, mean_recv).wait()
+    other_parts = part_all.at[pl.ds(0, count - 1)]
+    pltpu.make_async_copy(other_parts, other_parts, part_recv).wait()
+
+    per_core = data // cores
+    quad = jnp.zeros((2, 1), jnp.float32)
+    for core in range(cores):
+        blocks = []
+        for block in range(core * per_core, (core + 1) * per_core):
+            total = part_all[block * cores]
+            for other in range(1, cores):
+                total = total + part_all[block * cores + other]
+            image[block] = total
+            blocks.append(total)
+        half = jnp.concatenate(blocks, axis=1)
+        image_half[core] = half
+        quad = quad + jnp.sum(mean_all[core] * half, axis=1, keepdims=True)
+    coef = (1.0 - decay) / (decay * decay * (1.0 + (1.0 - decay) / decay * quad))
+    scaled = image[me_data] * coef
+    for side in range(2):
+        columns[side] = jnp.transpose(jnp.broadcast_to(scaled[side : side + 1, :], (128, rows)))
+
+    for side, buf in enumerate((l_buf, r_buf)):
+
+        def update(index, side=side, buf=buf):
+            piece = pl.ds(pl.multiple_of(index * step, step), step)
+            fresh = buf[piece, :] * (1.0 / decay) - (
+                columns[side, piece, :][:, 0:1] * image_half[me_core][side : side + 1, :]
+            )
+            buf[piece, :] = fresh
+            if side == 0:
+                l_panel[
+                    pl.ds(pl.multiple_of(me_inner * rows + index * step, step), step),
+                    pl.ds(pl.multiple_of(me_core * cols, cols), cols),
+                ] = fresh.astype(jnp.bfloat16)
+            else:
+                r_half[piece, :] = fresh.astype(jnp.bfloat16)
+
+        each(rows // step, update)
+
+    store_l = pltpu.make_async_copy(l_buf, new_l_ref, store_sem.at[0])
+    store_r = pltpu.make_async_copy(r_buf, new_r_ref, store_sem.at[1])
+    store_l.start()
+    store_r.start()
+
+    l_own = l_panel.at[
+        pl.ds(pl.multiple_of(me_inner * rows, rows), rows),
+        pl.ds(pl.multiple_of(me_core * cols, cols), cols),
+    ]
+    me_plane = me_inner * cores + me_core
+
+    def neighbour(index):
+        target = (me_plane + 1 + index) % plane
+        return me_outer * inner + target // cores, target % cores
+
+    def l_copy(index):
+        return remote(l_own, l_own, l_send.at[index], l_recv, *neighbour(index))
+
+    each(plane - 1, lambda index: l_copy(index).start())
+
+    slots = outer // cores
+    r_core = me_data // per_core
+    r_inner = (me_data % per_core) // slots
+    r_slot = me_data % slots
+    r_target = r_panel.at[
+        pl.ds(pl.multiple_of(r_slot * rows, rows), rows),
+        pl.ds(pl.multiple_of(me_core * cols, cols), cols),
+    ]
+    keeps = jnp.logical_and(r_core == me_core, r_inner == me_inner)
+    r_local = pltpu.make_async_copy(r_half, r_target, r_recv)
+
+    def r_copy(index):
+        target = (me_outer + 1 + index) % outer
+        return remote(
+            r_half, r_target, r_send.at[index], r_recv, target * inner + r_inner, r_core
+        )
+
+    each(outer - 1, lambda index: r_copy(index).start())
+
+    @pl.when(keeps)
+    def _():
+        r_local.start()
+
+    @pl.when(jnp.logical_not(keeps))
+    def _():
+        r_copy(outer - 1).start()
+
+    pltpu.make_async_copy(w_panel, w_panel, w_recv).wait()
+    other_l = l_panel.at[pl.ds(0, (plane - 1) * rows // cores), :]
+    pltpu.make_async_copy(other_l, other_l, l_recv).wait()
+
+    h_columns = pl.ds(pl.multiple_of(me_core * cols + me_inner * width, width), width)
+
+    def first(index):
+        piece = pl.ds(pl.multiple_of(index * rows, rows), rows)
+        h_panel[piece, h_columns] = jnp.dot(
+            l_panel[piece, :], w_panel[...], preferred_element_type=jnp.float32
+        ).astype(jnp.bfloat16)
+
+    each(inner, first)
+
+    h_own = h_panel.at[:, h_columns]
+
+    def h_copy(index):
+        return remote(h_own, h_own, h_send.at[index], h_recv, *neighbour(index))
+
+    each(plane - 1, lambda index: h_copy(index).start())
+
+    pltpu.make_async_copy(r_panel, r_panel, r_recv).wait()
+    other_h = h_panel.at[:, pl.ds(0, (plane - 1) * width)]
+    pltpu.make_async_copy(other_h, other_h, h_recv).wait()
+
+    out_columns = out_ref.at[:, pl.ds(pl.multiple_of(me_inner * width, width), width)]
+
+    def out_copy(index):
+        target = (me_inner + 1 + index) % inner
+        return remote(
+            result.at[pl.ds(pl.multiple_of(target * rows, rows), rows), :], out_columns,
+            out_send.at[index], out_recv, me_outer * inner + target, me_core,
+        )
+
+    out_own = pltpu.make_async_copy(
+        result.at[pl.ds(pl.multiple_of(me_inner * rows, rows), rows), :], out_columns, out_recv
+    )
+
+    def second(index):
+        target = (me_inner + 1 + index) % inner
+        piece = pl.ds(pl.multiple_of(target * rows, rows), rows)
+        result[piece, :] = lax.dot_general(
+            h_panel[piece, :], r_panel[...], (((1,), (1,)), ((), ())),
+            preferred_element_type=jnp.float32,
+        ).astype(jnp.bfloat16)
+
+        @pl.when(index < inner - 1)
+        def _():
+            out_copy(index).start()
+
+    each(inner, second)
+    out_own.start()
+
+    each(data - 1, lambda index: sums_copy(index).wait_send())
+    each(cores - 1, lambda index: mean_copy(index).wait_send())
+    each(count - 1, lambda index: part_copy(index).wait_send())
+    each(data - 1, lambda index: w_copy(index).wait_send())
+    each(plane - 1, lambda index: l_copy(index).wait_send())
+    each(outer - 1, lambda index: r_copy(index).wait_send())
+
+    @pl.when(jnp.logical_not(keeps))
+    def _():
+        r_copy(outer - 1).wait_send()
+
+    each(plane - 1, lambda index: h_copy(index).wait_send())
+    each(inner - 1, lambda index: out_copy(index).wait_send())
+    store_l.wait()
+    store_r.wait()
+    pltpu.make_async_copy(out_ref, out_ref, out_recv).wait()
+
+
+def fused(data, cores, layer_inputs, out_grads, weight_grad, left_inv, right_inv):
+    outer, inner = split(data)
+    plane = inner * cores
+    count = data * cores
+    rows, cols = left_inv.shape
+    width = cols // inner
+    tokens = layer_inputs.shape[0] * data
+    sums = jnp.stack(
+        [
+            jnp.sum(layer_inputs, axis=0, dtype=jnp.float32),
+            jnp.sum(out_grads, axis=0, dtype=jnp.float32),
+        ]
+    )
+    whole = pl.BlockSpec(memory_space=pl.ANY)
+    dma = pltpu.SemaphoreType.DMA
+    precond, new_left, new_right = pl.pallas_call(
+        functools.partial(kernel, outer, inner, cores, tokens),
+        out_shape=(
+            jax.ShapeDtypeStruct((rows, cols), jnp.bfloat16),
+            jax.ShapeDtypeStruct((rows, cols), jnp.float32),
+            jax.ShapeDtypeStruct((rows, cols), jnp.float32),
+        ),
+        in_specs=[pl.BlockSpec(memory_space=pltpu.VMEM), whole, whole, whole],
+        out_specs=(whole, whole, whole),
+        scratch_shapes=[
+            pltpu.VMEM((data, 2, cols), jnp.float32),
+            pltpu.VMEM((cores, 2, cols), jnp.float32),
+            pltpu.VMEM((count, 2, rows), jnp.float32),
+            pltpu.VMEM((data, 2, rows), jnp.float32),
+            pltpu.VMEM((cores, 2, cols), jnp.float32),
+            pltpu.VMEM((2, rows, 128), jnp.float32),
+            pltpu.VMEM((rows, cols), jnp.float32),
+            pltpu.VMEM((rows, cols), jnp.float32),
+            pltpu.VMEM((rows, cols), jnp.bfloat16),
+            pltpu.VMEM((data * rows, width), jnp.bfloat16),
+            pltpu.VMEM((inner * rows, cores * cols), jnp.bfloat16),
+            pltpu.VMEM((width, cores * cols), jnp.bfloat16),
+            pltpu.VMEM((inner * rows, cores * cols), jnp.bfloat16),
+            pltpu.VMEM((inner * rows, width), jnp.bfloat16),
+            dma((2,)),
+            dma((2,)),
+            dma((data,)),
+            dma((cores,)),
+            dma((count,)),
+            dma((data,)),
+            dma((plane,)),
+            dma((outer,)),
+            dma((plane,)),
+            dma((inner,)),
+        ]
+        + [dma(())] * 8,
+        compiler_params=pltpu.CompilerParams(
+            collective_id=0, has_side_effects=True, vmem_limit_bytes=60 * 1024 * 1024
+        ),
+        cost_estimate=pl.CostEstimate(
+            flops=4 * inner * rows * width * cores * cols,
+            bytes_accessed=16 * rows * cols,
+            transcendentals=0,
+        ),
+    )(sums, weight_grad, left_inv, jnp.transpose(right_inv))
+    return precond, new_left, jnp.transpose(new_right)
+
+
+def dispatch(data, cores, *arrays):
+    outer, inner = split(data)
+    rows, cols = arrays[3].shape
+    fits = (
+        cores > 1
+        and inner > 1
+        and outer % cores == 0
+        and rows % 32 == 0
+        and cols % (128 * inner) == 0
+        and cols * cores == rows * data
+    )
+    if fits:
+        return fused(data, cores, *arrays)
+    return gathered(*arrays)
+
+
 def solution(mesh):
     in_specs = (
         P("dp", "factor"),
@@ -73,5 +444,5 @@
     )
     out_specs = (P("dp", "factor"), P("dp", "factor"), P("factor", "dp"))
     return jax.shard_map(
-        per_device, mesh=mesh, in_specs=in_specs, out_specs=out_specs, check_vma=False
-    )
+        functools.partial(dispatch, mesh.shape["dp"], mesh.shape["factor"]), mesh=mesh, in_specs=in_specs, out_specs=out_specs, check_vma=False
+    )

time: 793 us -> 713 us (0.90)
  Pallas kernels: 0 us -> 695 us
  waiting for transfers between devices: 573 us -> 0 us
  blocking collectives: 153 us -> 0 us
  matrix products: 39.6 us -> 0 us
  between operations: 15.3 us -> 0.66 us
    pallas_call x0 -> x1, Pallas kernels: none -> 695 us  [fused(): pl.pallas_call(functools.partial(kernel, outer, inner, cores, tokens), ou...]
    all_gather x4 -> x0, waiting for transfers between devices: 572 us -> none  [the longest x1 284 us: per_device(): lax.all_gather(weight_grad, 'dp', axis=0, tiled=True)]
    psum x3 -> x0, blocking collectives: 135 us -> none  [the longest x1 60 us: per_device(): lax.psum((left_partial, right_partial), 'dp')]
    dot_general x6 -> x0, matrix products: 39.6 us -> none  [the longest x1 15.5 us: per_device(): jnp.dot(matched, lax.all_gather(weight_grad, 'dp', axis=0, tiled=True), p...]
    all_gather x2 -> x0, blocking collectives: 17.8 us -> none  [the longest x1 16 us: per_device(): lax.all_gather(mean_act, 'factor', axis=0, tiled=True)]
  transfers between devices with their start and end apart: 4 -> 0, of which waited for: 4 -> 0; matrix products, arithmetic and copies ran while one was open for 2% -> 0% of each run, Pallas kernels for 0% -> 0%
where the time goes in v1:
time: 713 us; the launch traced here: 709 us
  Pallas kernels  695 us (97%)
  local copies, waits for them, and re-layouts  8.3 us (1%)
    pallas_call x1, Pallas kernels, fused(): pl.pallas_call(functools.partial(kernel, outer, inner, cores, tokens), ou...  695 us

profile of v1, /device:TPU:3, one launch (start us, length us, event | category | flops | bytes accessed | tf_op | source)
XLA Modules:
  0.0 709.3 jit_solution(15081561222322936725)
XLA Ops:
  0.6 0.0 copy-start
  0.6 3.4 convert_reduce_fusion.1
  4.1 0.6 copy-done
  4.7 0.8 convert_reduce_fusion
  5.5 0.6 pad_maximum_fusion.sums_ref
  6.1 695.5 %shard_map.76 = (bf16[320,2560]{1,0:T(8,128)(2,1)}, f32[320,2560]{1,0:T(8,128)}, f32[320,2560]{1,0:T(8,128)}) custom-call(f32[2,2560]{1,0:T(2,128)} %pad_maximum_fusion.sums_ref, bf16[320,2560]{1,0:T(8,128)(2,1)} %w_ref.1, f32[320,2560]{1,0:T(8,128)} %l_ref.1, f32[320,2560]{1,0:T(8,128)} %bitcast.3), custom_call_target="tpu_custom_call" | custom-call | flops 16777216000 | bytes 13107200 | tf_op jit(solution)/shard_map/pallas_call | solution.py:373
  701.6 0.0 copy-start.2
  701.6 2.9 copy.11
  704.4 0.0 copy-done.2
  704.4 0.0 copy-start.1
  704.4 1.7 copy.12
  706.1 1.4 copy-done.1
  707.5 1.7 copy.13
  (2 shorter events, 0.0 us)
Async XLA Ops:
  0.6 4.0 copy-start
  701.6 2.9 copy-start.2
  704.4 3.1 copy-start.1

commit v2 on v1

--- a/solution.py
+++ b/solution.py
@@ -82,14 +82,15 @@
     sums_ref, w_ref, l_ref, r_ref,
     out_ref, new_l_ref, new_r_ref,
     sums_all, mean_all, part_all, image, image_half, columns,
-    l_buf, r_buf, r_half, w_panel, l_panel, r_panel, h_panel, result,
+    l_buf, r_buf, r_stage, w_panel, l_panel, r_panel, h_panel, result,
     load_sem, store_sem,
-    sums_send, mean_send, part_send, w_send, l_send, r_send, h_send, out_send,
-    sums_recv, mean_recv, part_recv, w_recv, l_recv, r_recv, h_recv, out_recv,
+    sums_send, mean_send, part_send, w_send, l_send, h_send, out_send,
+    wz_send, wz_recv, rz_send, rz_recv, lc_send, hc_send, rc_send,
+    sums_recv, mean_recv, part_recv, w_recv, l_recv, h_recv, out_recv, lc_recv, hc_recv, rc_recv,
 ):
     data = outer * inner
     count = data * cores
-    plane = inner * cores
+    slots = outer // cores
     rows, cols = l_buf.shape
     width = w_panel.shape[1]
     me_data = lax.axis_index("dp")
@@ -137,25 +138,57 @@
 
     each(data - 1, lambda index: sums_copy(index).start())
 
+    strip = inner * rows
+
+    def peer(index):
+        return me_outer * inner + (me_inner + 1 + index) % inner, me_core
+
+    def w_piece(block):
+        return w_ref.at[:, pl.ds(pl.multiple_of(block * width, width), width)]
+
+    w_place = w_panel.at[pl.ds(pl.multiple_of(me_data * rows, rows), rows), :]
+
     def w_copy(index):
-        target = (me_data + 1 + index) % data
-        return remote(
-            w_ref.at[:, pl.ds(pl.multiple_of((target % inner) * width, width), width)],
-            w_panel.at[pl.ds(pl.multiple_of(me_data * rows, rows), rows), :],
-            w_send.at[index], w_recv, target, me_core,
-        )
-
-    w_own = pltpu.make_async_copy(
-        w_ref.at[:, pl.ds(pl.multiple_of(me_inner * width, width), width)],
-        w_panel.at[pl.ds(pl.multiple_of(me_data * rows, rows), rows), :],
-        w_recv,
-    )
-
-    def start_w():
-        each(data - 1, lambda index: w_copy(index).start())
-        w_own.start()
-
-    start_w()
+        target = (me_inner + 1 + index) % inner
+        return remote(w_piece(target), w_place, w_send.at[index], w_recv, *peer(index))
+
+    def chain(step, block_of, send, recv, act):
+        right, left = me_outer - step, me_outer + step
+
+        @pl.when(jnp.logical_and(right >= 0, me_outer < outer - 1))
+        def _():
+            act(remote(
+                block_of(right), block_of(right), send.at[0, step], recv.at[right],
+                me_data + inner, me_core,
+            ))
+
+        @pl.when(jnp.logical_and(left < outer, me_outer > 0))
+        def _():
+            act(remote(
+                block_of(left), block_of(left), send.at[1, step], recv.at[left],
+                me_data - inner, me_core,
+            ))
+
+    def arrived(step, block_of, recv, after=None):
+        for block in (me_outer - 1 - step, me_outer + 1 + step):
+
+            @pl.when(jnp.logical_and(block >= 0, block < outer))
+            def _(block=block):
+                pltpu.make_async_copy(block_of(block), block_of(block), recv.at[block]).wait()
+                if after is not None:
+                    after(block)
+
+    def start(copy):
+        copy.start()
+
+    def w_block(block):
+        return w_panel.at[pl.ds(pl.multiple_of(block * strip, strip), strip), :]
+
+    def r_block(block):
+        return r_stage.at[block]
+
+    each(inner - 1, lambda index: w_copy(index).start())
+    pltpu.make_async_copy(w_piece(me_inner), w_place, w_recv).start()
 
     some = sums_all.at[pl.ds(0, data - 1)]
     pltpu.make_async_copy(some, some, sums_recv).wait()
@@ -200,6 +233,8 @@
     pltpu.make_async_copy(other_means, other_means, mean_recv).wait()
     other_parts = part_all.at[pl.ds(0, count - 1)]
     pltpu.make_async_copy(other_parts, other_parts, part_recv).wait()
+    pltpu.make_async_copy(w_block(me_outer), w_block(me_outer), w_recv).wait()
+    chain(0, w_block, wz_send, wz_recv, start)
 
     per_core = data // cores
     quad = jnp.zeros((2, 1), jnp.float32)
@@ -219,6 +254,12 @@
     for side in range(2):
         columns[side] = jnp.transpose(jnp.broadcast_to(scaled[side : side + 1, :], (128, rows)))
 
+    core_columns = pl.ds(pl.multiple_of(me_core * cols, cols), cols)
+    l_own = l_panel.at[pl.ds(pl.multiple_of(me_inner * rows, rows), rows), core_columns]
+
+    def l_copy(index):
+        return remote(l_own, l_own, l_send.at[index], l_recv, *peer(index))
+
     for side, buf in enumerate((l_buf, r_buf)):
 
         def update(index, side=side, buf=buf):
@@ -233,60 +274,58 @@
                     pl.ds(pl.multiple_of(me_core * cols, cols), cols),
                 ] = fresh.astype(jnp.bfloat16)
             else:
-                r_half[piece, :] = fresh.astype(jnp.bfloat16)
+                r_stage[me_outer, piece, :] = fresh.astype(jnp.bfloat16)
 
         each(rows // step, update)
+        if side == 0:
+            each(inner - 1, lambda index: l_copy(index).start())
 
     store_l = pltpu.make_async_copy(l_buf, new_l_ref, store_sem.at[0])
     store_r = pltpu.make_async_copy(r_buf, new_r_ref, store_sem.at[1])
     store_l.start()
     store_r.start()
 
-    l_own = l_panel.at[
-        pl.ds(pl.multiple_of(me_inner * rows, rows), rows),
-        pl.ds(pl.multiple_of(me_core * cols, cols), cols),
-    ]
-    me_plane = me_inner * cores + me_core
-
-    def neighbour(index):
-        target = (me_plane + 1 + index) % plane
-        return me_outer * inner + target // cores, target % cores
-
-    def l_copy(index):
-        return remote(l_own, l_own, l_send.at[index], l_recv, *neighbour(index))
-
-    each(plane - 1, lambda index: l_copy(index).start())
-
-    slots = outer // cores
-    r_core = me_data // per_core
-    r_inner = (me_data % per_core) // slots
-    r_slot = me_data % slots
-    r_target = r_panel.at[
-        pl.ds(pl.multiple_of(r_slot * rows, rows), rows),
-        pl.ds(pl.multiple_of(me_core * cols, cols), cols),
-    ]
-    keeps = jnp.logical_and(r_core == me_core, r_inner == me_inner)
-    r_local = pltpu.make_async_copy(r_half, r_target, r_recv)
-
-    def r_copy(index):
-        target = (me_outer + 1 + index) % outer
+    def core_copy(panel, send, recv, index):
+        slab = panel.at[:, core_columns]
+        return remote(slab, slab, send.at[index], recv, me_data, (me_core + 1 + index) % cores)
+
+    def whole_rows(panel, recv, send, recv_core, part):
+        pltpu.make_async_copy(part, part, recv).wait()
+        each(cores - 1, lambda index: core_copy(panel, send, recv_core, index).start())
+
+    def core_wait(panel, recv):
+        others = panel.at[:, pl.ds(0, (cores - 1) * cols)]
+        pltpu.make_async_copy(others, others, recv).wait()
+
+    def r_place(block):
+        return r_panel.at[
+            pl.ds(pl.multiple_of((block % slots) * rows, rows), rows), core_columns
+        ]
+
+    def r_relay(block):
         return remote(
-            r_half, r_target, r_send.at[index], r_recv, target * inner + r_inner, r_core
-        )
-
-    each(outer - 1, lambda index: r_copy(index).start())
-
-    @pl.when(keeps)
-    def _():
-        r_local.start()
-
-    @pl.when(jnp.logical_not(keeps))
-    def _():
-        r_copy(outer - 1).start()
-
-    pltpu.make_async_copy(w_panel, w_panel, w_recv).wait()
-    other_l = l_panel.at[pl.ds(0, (plane - 1) * rows // cores), :]
-    pltpu.make_async_copy(other_l, other_l, l_recv).wait()
+            r_block(block), r_place(block), rc_send.at[block], rc_recv, me_data, block // slots
+        )
+
+    def r_spread(block):
+        @pl.when(block // slots == me_core)
+        def _():
+            pltpu.make_async_copy(r_block(block), r_place(block), rc_recv).start()
+
+        @pl.when(block // slots != me_core)
+        def _():
+            r_relay(block).start()
+
+    for step_z in range(1, outer - 1):
+        arrived(step_z - 1, w_block, wz_recv)
+        chain(step_z, w_block, wz_send, wz_recv, start)
+    whole_rows(
+        l_panel, l_recv, lc_send, lc_recv, l_panel.at[pl.ds(0, (inner - 1) * rows), core_columns]
+    )
+    arrived(outer - 2, w_block, wz_recv)
+    chain(0, r_block, rz_send, rz_recv, start)
+    r_spread(me_outer)
+    core_wait(l_panel, lc_recv)
 
     h_columns = pl.ds(pl.multiple_of(me_core * cols + me_inner * width, width), width)
 
@@ -301,25 +340,31 @@
     h_own = h_panel.at[:, h_columns]
 
     def h_copy(index):
-        return remote(h_own, h_own, h_send.at[index], h_recv, *neighbour(index))
-
-    each(plane - 1, lambda index: h_copy(index).start())
-
-    pltpu.make_async_copy(r_panel, r_panel, r_recv).wait()
-    other_h = h_panel.at[:, pl.ds(0, (plane - 1) * width)]
-    pltpu.make_async_copy(other_h, other_h, h_recv).wait()
-
-    out_columns = out_ref.at[:, pl.ds(pl.multiple_of(me_inner * width, width), width)]
+        return remote(h_own, h_own, h_send.at[index], h_recv, *peer(index))
+
+    each(inner - 1, lambda index: h_copy(index).start())
+
+    for step_z in range(1, outer - 1):
+        arrived(step_z - 1, r_block, rz_recv, r_spread)
+        chain(step_z, r_block, rz_send, rz_recv, start)
+    whole_rows(
+        h_panel, h_recv, hc_send, hc_recv, h_panel.at[:, pl.ds(0, (inner - 1) * width)]
+    )
+    arrived(outer - 2, r_block, rz_recv, r_spread)
+    pltpu.make_async_copy(r_panel, r_panel, rc_recv).wait()
+    core_wait(h_panel, hc_recv)
+
+    out_place = out_ref.at[me_inner]
 
     def out_copy(index):
         target = (me_inner + 1 + index) % inner
         return remote(
-            result.at[pl.ds(pl.multiple_of(target * rows, rows), rows), :], out_columns,
+            result.at[pl.ds(pl.multiple_of(target * rows, rows), rows), :], out_place,
             out_send.at[index], out_recv, me_outer * inner + target, me_core,
         )
 
     out_own = pltpu.make_async_copy(
-        result.at[pl.ds(pl.multiple_of(me_inner * rows, rows), rows), :], out_columns, out_recv
+        result.at[pl.ds(pl.multiple_of(me_inner * rows, rows), rows), :], out_place, out_recv
     )
 
     def second(index):
@@ -340,16 +385,21 @@
     each(data - 1, lambda index: sums_copy(index).wait_send())
     each(cores - 1, lambda index: mean_copy(index).wait_send())
     each(count - 1, lambda index: part_copy(index).wait_send())
-    each(data - 1, lambda index: w_copy(index).wait_send())
-    each(plane - 1, lambda index: l_copy(index).wait_send())
-    each(outer - 1, lambda index: r_copy(index).wait_send())
-
-    @pl.when(jnp.logical_not(keeps))
-    def _():
-        r_copy(outer - 1).wait_send()
-
-    each(plane - 1, lambda index: h_copy(index).wait_send())
+    each(inner - 1, lambda index: w_copy(index).wait_send())
+    each(inner - 1, lambda index: l_copy(index).wait_send())
+    each(inner - 1, lambda index: h_copy(index).wait_send())
     each(inner - 1, lambda index: out_copy(index).wait_send())
+    each(cores - 1, lambda index: core_copy(l_panel, lc_send, lc_recv, index).wait_send())
+    each(cores - 1, lambda index: core_copy(h_panel, hc_send, hc_recv, index).wait_send())
+    for step_z in range(outer - 1):
+        chain(step_z, w_block, wz_send, wz_recv, lambda copy: copy.wait_send())
+        chain(step_z, r_block, rz_send, rz_recv, lambda copy: copy.wait_send())
+    for block in range(outer):
+
+        @pl.when(block // slots != me_core)
+        def _(block=block):
+            r_relay(block).wait_send()
+
     store_l.wait()
     store_r.wait()
     pltpu.make_async_copy(out_ref, out_ref, out_recv).wait()
@@ -357,7 +407,6 @@
 
 def fused(data, cores, layer_inputs, out_grads, weight_grad, left_inv, right_inv):
     outer, inner = split(data)
-    plane = inner * cores
     count = data * cores
     rows, cols = left_inv.shape
     width = cols // inner
@@ -373,7 +422,7 @@
     precond, new_left, new_right = pl.pallas_call(
         functools.partial(kernel, outer, inner, cores, tokens),
         out_shape=(
-            jax.ShapeDtypeStruct((rows, cols), jnp.bfloat16),
+            jax.ShapeDtypeStruct((inner, rows, width), jnp.bfloat16),
             jax.ShapeDtypeStruct((rows, cols), jnp.float32),
             jax.ShapeDtypeStruct((rows, cols), jnp.float32),
         ),
@@ -388,7 +437,7 @@
             pltpu.VMEM((2, rows, 128), jnp.float32),
             pltpu.VMEM((rows, cols), jnp.float32),
             pltpu.VMEM((rows, cols), jnp.float32),
-            pltpu.VMEM((rows, cols), jnp.bfloat16),
+            pltpu.VMEM((outer, rows, cols), jnp.bfloat16),
             pltpu.VMEM((data * rows, width), jnp.bfloat16),
             pltpu.VMEM((inner * rows, cores * cols), jnp.bfloat16),
             pltpu.VMEM((width, cores * cols), jnp.bfloat16),
@@ -399,13 +448,19 @@
             dma((data,)),
             dma((cores,)),
             dma((count,)),
-            dma((data,)),
-            dma((plane,)),
+            dma((inner,)),
+            dma((inner,)),
+            dma((inner,)),
+            dma((inner,)),
+            dma((2, outer)),
             dma((outer,)),
-            dma((plane,)),
-            dma((inner,)),
+            dma((2, outer)),
+            dma((outer,)),
+            dma((cores,)),
+            dma((cores,)),
+            dma((outer,)),
         ]
-        + [dma(())] * 8,
+        + [dma(())] * 10,
         compiler_params=pltpu.CompilerParams(
             collective_id=0, has_side_effects=True, vmem_limit_bytes=60 * 1024 * 1024
         ),
@@ -415,6 +470,8 @@
             transcendentals=0,
         ),
     )(sums, weight_grad, left_inv, jnp.transpose(right_inv))
+    precond = precond.reshape(inner, rows, width // rows, rows)
+    precond = jnp.transpose(precond, (1, 2, 0, 3)).reshape(rows, cols)
     return precond, new_left, jnp.transpose(new_right)
 
 

time: 713 us -> 296 us (0.42)
  Pallas kernels: 695 us -> 271 us
  local copies, waits for them, and re-layouts: 8.3 us -> 18.4 us
    pallas_call x1, Pallas kernels: 695 us -> 271 us  [fused(): pl.pallas_call(functools.partial(kernel, outer, inner, cores, tokens), ou...]
    reshape x0 -> x2, local copies, waits for them, and re-layouts: none -> 9.13 us  [the longest x1 4.73 us: fused(): precond = jnp.transpose(precond, (1, 2, 0, 3)).reshape(rows, cols)]
where the time goes in v2:
time: 296 us; the launch traced here: 295 us
  Pallas kernels  271 us (92%)
  local copies, waits for them, and re-layouts  18.4 us (6%)
  other arithmetic  4.81 us (2%)
    pallas_call x1, Pallas kernels, fused(): pl.pallas_call(functools.partial(kernel, outer, inner, cores, tokens), ou...  271 us

profile of v2, /device:TPU:3, one launch (start us, length us, event | category | flops | bytes accessed | tf_op | source)
XLA Modules:
  0.0 295.3 jit_solution(2357582404697661337)
XLA Ops:
  0.6 0.0 copy-start
  0.6 3.4 %convert_reduce_fusion.1 = f32[2560]{0:T(1024)S(1)} fusion(bf16[1024,2560]{1,0:T(8,128)(2,1)} %param.5), kind=kLoop, calls=%fused_computation.1 | loop fusion | flops 5240320 | bytes 5253120 | tf_op jit(solution)/shard_map/reduce_sum | solution.py:416
  4.1 0.6 copy-done
  4.7 0.8 convert_reduce_fusion
  5.5 0.6 pad_maximum_fusion.sums_ref
  6.1 271.5 %shard_map.76 = (bf16[4,320,640]{2,1,0:T(8,128)(2,1)}, f32[320,2560]{1,0:T(8,128)}, f32[320,2560]{1,0:T(8,128)}) custom-call(f32[2,2560]{1,0:T(2,128)} %pad_maximum_fusion.sums_ref, bf16[320,2560]{1,0:T(8,128)(2,1)} %w_ref.1, f32[320,2560]{1,0:T(8,128)} %l_ref.1, f32[320,2560]{1,0:T(8,128)} %bitcast.5), custom_call_target="tpu_custom_call" | custom-call | flops 16777216000 | bytes 13107200 | tf_op jit(solution)/shard_map/pallas_call | solution.py:422
  277.6 4.4 %reshape.12 = bf16[4,320,2,320]{3,2,1,0:T(2,128)(2,1)S(1)} reshape(bf16[4,320,640]{2,1,0:T(8,128)(2,1)} %get-tuple-element.6) | data formatting | bytes 3276800 | tf_op jit(solution)/shard_map/reshape | solution.py:473
  282.0 3.8 %copy.8 = bf16[320,2,4,320]{3,2,1,0:T(4,128)(2,1)} copy(bf16[320,2,4,320]{3,1,0,2:T(2,128)(2,1)S(1)} %bitcast.3) | data formatting | bytes 3276800 | tf_op jit(solution)/shard_map/transpose | solution.py:474
  285.8 0.0 copy-start.2
  285.8 4.7 %reshape.13 = bf16[320,2560]{1,0:T(8,128)(2,1)} reshape(bf16[320,2,4,320]{3,2,1,0:T(4,128)(2,1)} %copy.8) | data formatting | bytes 3276800 | tf_op jit(solution)/shard_map/reshape | solution.py:474
  290.5 0.0 copy-done.2
  290.5 0.0 copy-start.1
  290.5 1.7 copy.11
  292.2 1.4 copy-done.1
  293.6 1.7 copy.12
  (2 shorter events, 0.0 us)
Async XLA Ops:
  0.6 4.0 %copy-start = (bf16[1024,2560]{1,0:T(8,128)(2,1)S(1)}, bf16[1024,2560]{1,0:T(8,128)(2,1)}, u32[]{:S(2)}) copy-start(bf16[1024,2560]{1,0:T(8,128)(2,1)} %param.6) | copy-start | bytes 15728644
  285.8 4.7 %copy-start.2 = (f32[320,2560]{1,0:T(8,128)S(1)}, f32[320,2560]{1,0:T(8,128)}, u32[]{:S(2)}) copy-start(f32[320,2560]{1,0:T(8,128)} %get-tuple-element.13) | copy-start | bytes 9830404
  290.5 3.1 %copy-start.1 = (f32[320,2560]{1,0:T(8,128)S(1)}, f32[320,2560]{1,0:T(8,128)}, u32[]{:S(2)}) copy-start(f32[320,2560]{1,0:T(8,128)} %get-tuple-element.8) | copy-start | bytes 9830404

commit v3 on v2

--- a/solution.py
+++ b/solution.py
@@ -79,10 +79,10 @@
 
 def kernel(
     outer, inner, cores, tokens,
-    sums_ref, w_ref, l_ref, r_ref,
+    x_ref, g_ref, w_ref, l_ref, r_ref,
     out_ref, new_l_ref, new_r_ref,
     sums_all, mean_all, part_all, image, image_half, columns,
-    l_buf, r_buf, r_stage, w_panel, l_panel, r_panel, h_panel, result,
+    l_buf, r_buf, r_stage, w_panel, l_panel, r_panel, h_panel, result, pieces,
     load_sem, store_sem,
     sums_send, mean_send, part_send, w_send, l_send, h_send, out_send,
     wz_send, wz_recv, rz_send, rz_recv, lc_send, hc_send, rc_send,
@@ -112,11 +112,19 @@
 
         lax.fori_loop(0, total, step, 0)
 
+    token_rows = x_ref.shape[0]
+    tokens_in = [
+        pltpu.make_async_copy(
+            ref, h_panel.at[pl.ds(0, token_rows), pl.ds(side * cols, cols)], load_sem.at[2 + side]
+        )
+        for side, ref in enumerate((x_ref, g_ref))
+    ]
+    for load in tokens_in:
+        load.start()
     load_l = pltpu.make_async_copy(l_ref, l_buf, load_sem.at[0])
     load_r = pltpu.make_async_copy(r_ref, r_buf, load_sem.at[1])
     load_l.start()
     load_r.start()
-    sums_all[me_data] = sums_ref[...]
 
     barrier = pltpu.get_barrier_semaphore()
 
@@ -135,8 +143,6 @@
             sums_all.at[me_data], sums_all.at[me_data],
             sums_send.at[index], sums_recv, target, me_core,
         )
-
-    each(data - 1, lambda index: sums_copy(index).start())
 
     strip = inner * rows
 
@@ -190,6 +196,26 @@
     each(inner - 1, lambda index: w_copy(index).start())
     pltpu.make_async_copy(w_piece(me_inner), w_place, w_recv).start()
 
+    for side in range(2):
+        tokens_in[side].wait()
+        for block in range(inner):
+            first_column = side * cols + block * width
+
+            def add(index, total, first_column=first_column):
+                piece = h_panel[
+                    pl.ds(pl.multiple_of(index * 64, 64), 64), pl.ds(first_column, width)
+                ].astype(jnp.float32)
+                return total + jnp.sum(piece.reshape(8, 8, width), axis=0)
+
+            total = lax.fori_loop(
+                0, token_rows // 64, add, jnp.zeros((8, width), jnp.float32)
+            )
+            sums_all[me_data, side : side + 1, pl.ds(block * width, width)] = jnp.sum(
+                total, axis=0, keepdims=True
+            )
+
+    each(data - 1, lambda index: sums_copy(index).start())
+
     some = sums_all.at[pl.ds(0, data - 1)]
     pltpu.make_async_copy(some, some, sums_recv).wait()
     mean = jnp.sum(sums_all[...], axis=0) / tokens
@@ -229,12 +255,13 @@
 
     each(count - 1, lambda index: part_copy(index).start())
 
+    pltpu.make_async_copy(w_block(me_outer), w_block(me_outer), w_recv).wait()
+    chain(0, w_block, wz_send, wz_recv, start)
+
     other_means = mean_all.at[pl.ds(0, cores - 1)]
     pltpu.make_async_copy(other_means, other_means, mean_recv).wait()
     other_parts = part_all.at[pl.ds(0, count - 1)]
     pltpu.make_async_copy(other_parts, other_parts, part_recv).wait()
-    pltpu.make_async_copy(w_block(me_outer), w_block(me_outer), w_recv).wait()
-    chain(0, w_block, wz_send, wz_recv, start)
 
     per_core = data // cores
     quad = jnp.zeros((2, 1), jnp.float32)
@@ -329,32 +356,50 @@
 
     h_columns = pl.ds(pl.multiple_of(me_core * cols + me_inner * width, width), width)
 
+    def tile(index):
+        return pl.ds(pl.multiple_of(index * rows, rows), rows)
+
+    def h_copy(index, other):
+        own = h_panel.at[tile(index), h_columns]
+        return remote(own, own, h_send.at[index, other], h_recv.at[index], *peer(other))
+
+    def h_core(index, other):
+        slab = h_panel.at[tile(index), core_columns]
+        return remote(
+            slab, slab, hc_send.at[index, other], hc_recv.at[index],
+            me_data, (me_core + 1 + other) % cores,
+        )
+
     def first(index):
-        piece = pl.ds(pl.multiple_of(index * rows, rows), rows)
+        piece = tile(index)
         h_panel[piece, h_columns] = jnp.dot(
             l_panel[piece, :], w_panel[...], preferred_element_type=jnp.float32
         ).astype(jnp.bfloat16)
+        for other in range(inner - 1):
+            h_copy(index, other).start()
+
+    def pass_on(index):
+        peers = h_panel.at[tile(index), pl.ds(0, (inner - 1) * width)]
+        pltpu.make_async_copy(peers, peers, h_recv.at[index]).wait()
+        for other in range(cores - 1):
+            h_core(index, other).start()
+
+    def h_done(index):
+        for other in range(inner - 1):
+            h_copy(index, other).wait_send()
+        for other in range(cores - 1):
+            h_core(index, other).wait_send()
 
     each(inner, first)
-
-    h_own = h_panel.at[:, h_columns]
-
-    def h_copy(index):
-        return remote(h_own, h_own, h_send.at[index], h_recv, *peer(index))
-
-    each(inner - 1, lambda index: h_copy(index).start())
 
     for step_z in range(1, outer - 1):
         arrived(step_z - 1, r_block, rz_recv, r_spread)
         chain(step_z, r_block, rz_send, rz_recv, start)
-    whole_rows(
-        h_panel, h_recv, hc_send, hc_recv, h_panel.at[:, pl.ds(0, (inner - 1) * width)]
-    )
+    each(inner, pass_on)
     arrived(outer - 2, r_block, rz_recv, r_spread)
     pltpu.make_async_copy(r_panel, r_panel, rc_recv).wait()
-    core_wait(h_panel, hc_recv)
-
-    out_place = out_ref.at[me_inner]
+
+    out_place = pieces.at[me_inner]
 
     def out_copy(index):
         target = (me_inner + 1 + index) % inner
@@ -369,7 +414,9 @@
 
     def second(index):
         target = (me_inner + 1 + index) % inner
-        piece = pl.ds(pl.multiple_of(target * rows, rows), rows)
+        piece = tile(target)
+        others = h_panel.at[piece, pl.ds(0, (cores - 1) * cols)]
+        pltpu.make_async_copy(others, others, hc_recv.at[target]).wait()
         result[piece, :] = lax.dot_general(
             h_panel[piece, :], r_panel[...], (((1,), (1,)), ((), ())),
             preferred_element_type=jnp.float32,
@@ -387,10 +434,9 @@
     each(count - 1, lambda index: part_copy(index).wait_send())
     each(inner - 1, lambda index: w_copy(index).wait_send())
     each(inner - 1, lambda index: l_copy(index).wait_send())
-    each(inner - 1, lambda index: h_copy(index).wait_send())
+    each(inner, h_done)
     each(inner - 1, lambda index: out_copy(index).wait_send())
     each(cores - 1, lambda index: core_copy(l_panel, lc_send, lc_recv, index).wait_send())
-    each(cores - 1, lambda index: core_copy(h_panel, hc_send, hc_recv, index).wait_send())
     for step_z in range(outer - 1):
         chain(step_z, w_block, wz_send, wz_recv, lambda copy: copy.wait_send())
         chain(step_z, r_block, rz_send, rz_recv, lambda copy: copy.wait_send())
@@ -402,7 +448,20 @@
 
     store_l.wait()
     store_r.wait()
-    pltpu.make_async_copy(out_ref, out_ref, out_recv).wait()
+    pltpu.make_async_copy(pieces, pieces, out_recv).wait()
+
+    def assemble(index):
+        piece = pl.ds(pl.multiple_of(index * step, step), step)
+        parts = [pieces[block, piece, :] for block in range(inner)]
+        r_stage[0, piece, :] = jnp.concatenate(
+            [part[:, slot * rows : (slot + 1) * rows] for slot in range(slots) for part in parts],
+            axis=1,
+        )
+
+    each(rows // step, assemble)
+    store_out = pltpu.make_async_copy(r_stage.at[0], out_ref, store_sem.at[2])
+    store_out.start()
+    store_out.wait()
 
 
 def fused(data, cores, layer_inputs, out_grads, weight_grad, left_inv, right_inv):
@@ -411,22 +470,16 @@
     rows, cols = left_inv.shape
     width = cols // inner
     tokens = layer_inputs.shape[0] * data
-    sums = jnp.stack(
-        [
-            jnp.sum(layer_inputs, axis=0, dtype=jnp.float32),
-            jnp.sum(out_grads, axis=0, dtype=jnp.float32),
-        ]
-    )
     whole = pl.BlockSpec(memory_space=pl.ANY)
     dma = pltpu.SemaphoreType.DMA
     precond, new_left, new_right = pl.pallas_call(
         functools.partial(kernel, outer, inner, cores, tokens),
         out_shape=(
-            jax.ShapeDtypeStruct((inner, rows, width), jnp.bfloat16),
+            jax.ShapeDtypeStruct((rows, cols), jnp.bfloat16),
             jax.ShapeDtypeStruct((rows, cols), jnp.float32),
             jax.ShapeDtypeStruct((rows, cols), jnp.float32),
         ),
-        in_specs=[pl.BlockSpec(memory_space=pltpu.VMEM), whole, whole, whole],
+        in_specs=[whole] * 5,
         out_specs=(whole, whole, whole),
         scratch_shapes=[
             pltpu.VMEM((data, 2, cols), jnp.float32),
@@ -443,35 +496,43 @@
             pltpu.VMEM((width, cores * cols), jnp.bfloat16),
             pltpu.VMEM((inner * rows, cores * cols), jnp.bfloat16),
             pltpu.VMEM((inner * rows, width), jnp.bfloat16),
-            dma((2,)),
-            dma((2,)),
+            pltpu.VMEM((inner, rows, width), jnp.bfloat16),
+            dma((4,)),
+            dma((3,)),
             dma((data,)),
             dma((cores,)),
             dma((count,)),
             dma((inner,)),
             dma((inner,)),
-            dma((inner,)),
+            dma((inner, inner)),
             dma((inner,)),
             dma((2, outer)),
             dma((outer,)),
             dma((2, outer)),
             dma((outer,)),
             dma((cores,)),
-            dma((cores,)),
+            dma((inner, cores)),
             dma((outer,)),
-        ]
-        + [dma(())] * 10,
+            dma(()),
+            dma(()),
+            dma(()),
+            dma(()),
+            dma(()),
+            dma((inner,)),
+            dma(()),
+            dma(()),
+            dma((inner,)),
+            dma(()),
+        ],
         compiler_params=pltpu.CompilerParams(
-            collective_id=0, has_side_effects=True, vmem_limit_bytes=60 * 1024 * 1024
+            collective_id=0, has_side_effects=True, vmem_limit_bytes=62 * 1024 * 1024
         ),
         cost_estimate=pl.CostEstimate(
             flops=4 * inner * rows * width * cores * cols,
             bytes_accessed=16 * rows * cols,
             transcendentals=0,
         ),
-    )(sums, weight_grad, left_inv, jnp.transpose(right_inv))
-    precond = precond.reshape(inner, rows, width // rows, rows)
-    precond = jnp.transpose(precond, (1, 2, 0, 3)).reshape(rows, cols)
+    )(layer_inputs, out_grads, weight_grad, left_inv, jnp.transpose(right_inv))
     return precond, new_left, jnp.transpose(new_right)
 
 
@@ -483,6 +544,8 @@
         and inner > 1
         and outer % cores == 0
         and rows % 32 == 0
+        and arrays[0].shape[0] % 64 == 0
+        and arrays[0].shape[0] <= inner * rows
         and cols % (128 * inner) == 0
         and cols * cores == rows * data
     )

time: 296 us -> 284 us (0.959)
  local copies, waits for them, and re-layouts: 18.4 us -> 7.67 us
  Pallas kernels: 271 us -> 276 us
  other arithmetic: 4.81 us -> 0 us
    reshape x2 -> x0, local copies, waits for them, and re-layouts: 9.13 us -> none  [the longest x1 4.73 us: fused(): precond = jnp.transpose(precond, (1, 2, 0, 3)).reshape(rows, cols)]
    reduce_sum x2 -> x0, other arithmetic: 4.18 us -> none  [the longest x1 3.41 us: fused(): jnp.sum(layer_inputs, axis=0, dtype=jnp.float32)]
    pallas_call x1, Pallas kernels: 271 us -> 276 us  [fused(): pl.pallas_call(functools.partial(kernel, outer, inner, cores, tokens), ou...]
    transpose x1 -> x0, local copies, waits for them, and re-layouts: 3.8 us -> none  [fused(): precond = jnp.transpose(precond, (1, 2, 0, 3)).reshape(rows, cols)]
    unnamed x8 -> x7, local copies, waits for them, and re-layouts: 5.43 us -> 7.67 us
where the time goes in v3:
time: 284 us
  Pallas kernels  276 us (97%)
  local copies, waits for them, and re-layouts  7.67 us (3%)
    pallas_call x1, Pallas kernels, fused(): pl.pallas_call(functools.partial(kernel, outer, inner, cores, tokens), ou...  276 us
    unnamed x7, local copies, waits for them, and re-layouts  7.67 us

profile of v3, /device:TPU:3, one launch (start us, length us, event | category | flops | bytes accessed | tf_op | source)
XLA Modules:
  0.0 283.8 jit_solution(335570713951520993)
XLA Ops:
  0.6 275.5 %shard_map.76 = (bf16[320,2560]{1,0:T(8,128)(2,1)}, f32[320,2560]{1,0:T(8,128)}, f32[320,2560]{1,0:T(8,128)}) custom-call(bf16[1024,2560]{1,0:T(8,128)(2,1)} %x_ref.1, bf16[1024,2560]{1,0:T(8,128)(2,1)} %g_ref.1, bf16[320,2560]{1,0:T(8,128)(2,1)} %w_ref.1, f32[320,2560]{1,0:T(8,128)} %l_ref.1, f32[320,2560]{1,0:T(8,128)} %bitcast.3), custom_call_target="tpu_custom_call" | custom-call | flops 16777216000 | bytes 13107200 | tf_op jit(solution)/shard_map/pallas_call | solution.py:475
  276.1 0.0 copy-start.1
  276.2 2.9 %copy.11 = bf16[320,2560]{1,0:T(8,128)(2,1)} copy(bf16[320,2560]{1,0:T(8,128)(2,1)} %get-tuple-element.12) | data formatting | bytes 3276800
  279.0 0.0 copy-done.1
  279.0 0.0 copy-start
  279.0 1.7 copy.12
  280.7 1.4 copy-done
  282.1 1.7 copy.13
Async XLA Ops:
  276.1 2.9 %copy-start.1 = (f32[320,2560]{1,0:T(8,128)S(1)}, f32[320,2560]{1,0:T(8,128)}, u32[]{:S(2)}) copy-start(f32[320,2560]{1,0:T(8,128)} %get-tuple-element.13) | copy-start | bytes 9830404
  279.0 3.1 %copy-start = (f32[320,2560]{1,0:T(8,128)S(1)}, f32[320,2560]{1,0:T(8,128)}, u32[]{:S(2)}) copy-start(f32[320,2560]{1,0:T(8,128)} %get-tuple-element.8) | copy-start | bytes 9830404
